TPU v7x, 32 devices: a whole 2x2x4 slice. The times are simulated.
32 devices in a mesh: groups: 2 (over y), ctx: 4 (over z), head: 2 (over x), section: 2 (over core).
Axes of the slice: x: 2, y: 2, z: 4, core: 2. Of those that a mesh axis runs over, the one named last changes fastest.
Arguments:
- tokens: bfloat16 [1024, 8192], P(('groups', 'ctx'), ('head', 'section')), parts along dimension 0, may hold values from -6 to 6
- norm_gain: bfloat16 [8192], replicated, may hold values from 0.099609375 to 1.8984375
- w_qkv: bfloat16 [8192, 10240], P('ctx', ('head', 'section')), may hold values from -0.0625 to 0.0625
- prefix_kv: bfloat16 [4096, 8, 256], P(('groups', 'ctx'), ('head', 'section')), parts along dimension 0, may hold values from -200 to 200
- prefix_counts: int32 [8], P(('groups', 'ctx')), parts along dimension 0, may hold values from 0 to 4, as said below
- span_offset: int32 [2], P('groups'), parts along dimension 0, may hold values from 32 to 95
- handoff_slots: int32 [8], P(('groups', 'ctx')), parts along dimension 0, may hold values from 0 to 15, as said below
Outputs:
- attended: bfloat16 [1024, 8192], P(('groups', 'ctx'), ('head', 'section')), parts along dimension 0
- decode_cache: bfloat16 [4096, 8, 256], P(('groups', 'ctx'), ('head', 'section')), parts along dimension 0
There are 2 independent parts, one for each index of `groups`. A program takes and returns all parts, laid end to end along the dimension named above; an argument that names none is the same for every part. Nothing has to cross between parts.
Inputs may be any that keep to these rules, and one draw needn't show every extreme that they name: `prefix_counts`: some index of ctx holds all 4 blocks. `handoff_slots`: distinct values; slot s belongs to index s // 4 of ctx; a quarter of the indices of ctx receive blocks, each of them in all of its 4 slots.
All inputs are finite; a program needn't handle non-finite values.
Results may differ from a plain program's by a relative error of at most 0.007.
The roundings to bfloat16 on the way count: a program that leaves them out, or rounds other values in their place, can miss the bound.
Values may be sent and summed in bfloat16 or wider, within the bound.
A program may use at most 128 MiB of HBM per device.

v0:
```python
import math

import jax
import jax.numpy as jnp
from jax import lax
from jax.sharding import PartitionSpec as P

HEAD_DIM = 128
GROUP = 8
BLK = 128


ROPE_BASE = 500000.0
NORM_EPS = 1e-05


def rotate(vectors, positions):
    half_dim = vectors.shape[-1] // 2
    frequency = ROPE_BASE ** (-(jnp.arange(half_dim, dtype=jnp.float32) * 2.0) / vectors.shape[-1])
    angles = positions[:, None] * frequency[None, :]
    view_shape = (vectors.shape[0],) + (1,) * (vectors.ndim - 2) + (half_dim,)
    cosines = jnp.cos(angles).reshape(view_shape)
    sine_part = jnp.sin(angles).reshape(view_shape)
    lower_part = vectors[..., :half_dim]
    upper_part = vectors[..., half_dim:]
    return jnp.concatenate(
        [
            lower_part * cosines - upper_part * sine_part,
            upper_part * cosines + lower_part * sine_part,
        ],
        -1,
    )


def fresh_state(row_count, head_count):
    return (
        jnp.full((row_count, head_count, GROUP), -1e30, jnp.float32),
        jnp.zeros((row_count, head_count, GROUP), jnp.float32),
        jnp.zeros((row_count, head_count, GROUP, HEAD_DIM), jnp.float32),
    )


def advance(states_now, query_set, key_rows, value_rows, visible):
    running_max, totals, weighted_sum = states_now
    scores = jnp.einsum(
        "rhgd,khd->rhgk", query_set, key_rows, preferred_element_type=jnp.float32
    ) * (1.0 / math.sqrt(HEAD_DIM))
    visible_map = visible[:, None, None, :]
    new_max = jnp.maximum(running_max, jnp.max(jnp.where(visible_map, scores, -1e30), -1))
    shrink_by = jnp.exp(running_max - new_max)
    weights = jnp.where(visible_map, jnp.exp(scores - new_max[..., None]), 0.0)
    totals = totals * shrink_by + jnp.sum(weights, -1)
    weighted_sum = weighted_sum * shrink_by[..., None] + jnp.einsum(
        "rhgk,khd->rhgd",
        weights.astype(jnp.bfloat16),
        value_rows,
        preferred_element_type=jnp.float32,
    )
    return (new_max, totals, weighted_sum)


def finish(states_now):
    running_max, totals, weighted_sum = states_now
    blended = weighted_sum / totals[..., None]
    return blended.reshape(blended.shape[0], -1).astype(jnp.bfloat16)


def local(tokens, norm_gain, w_qkv, prefix_kv, prefix_counts, span_offset, handoff_slots):
    row_count = tokens.shape[0]
    device = lax.axis_index("ctx")
    features = lax.all_gather(tokens, ("head", "section"), axis=1, tiled=True)
    values = features.astype(jnp.float32)
    scale_row = lax.rsqrt(jnp.mean(values * values, -1, keepdims=True) + NORM_EPS)
    normed = (values * scale_row * norm_gain.astype(jnp.float32)).astype(jnp.bfloat16)
    proj_width = w_qkv.shape[1]
    projected = jnp.dot(
        normed, lax.all_gather(w_qkv, "ctx", axis=0, tiled=True), preferred_element_type=jnp.float32
    )
    head_count = proj_width // ((GROUP + 2) * HEAD_DIM)
    projected = projected.reshape(row_count, head_count, GROUP + 2, HEAD_DIM)
    local_pos = device * row_count + jnp.arange(row_count, dtype=jnp.int32)
    positions = (span_offset[0] * BLK + local_pos).astype(jnp.float32)
    queries = rotate(projected[:, :, :GROUP], positions).astype(jnp.bfloat16)
    keys_new = rotate(projected[:, :, GROUP], positions).astype(jnp.bfloat16)
    values_new = projected[:, :, GROUP + 1].astype(jnp.bfloat16)
    new_pairs = jnp.concatenate([keys_new, values_new], -1)
    live_rows = (jnp.arange(prefix_kv.shape[0], dtype=jnp.int32) < prefix_counts[0] * BLK).astype(
        jnp.int32
    )
    targets = jnp.repeat(handoff_slots, BLK)
    half_rows = row_count // 2
    lower_queries = queries[:half_rows]
    upper_queries = queries[half_rows:]
    lower_pos = device * row_count + jnp.arange(half_rows, dtype=jnp.int32)
    upper_pos = device * row_count + half_rows + jnp.arange(half_rows, dtype=jnp.int32)
    begun = (fresh_state(half_rows, head_count), fresh_state(half_rows, head_count))
    pairs_in = lax.all_gather(prefix_kv, "ctx", axis=0, tiled=True)
    flags_in = lax.all_gather(live_rows, "ctx", axis=0, tiled=True)
    key_rows = pairs_in[..., :HEAD_DIM]
    value_rows = pairs_in[..., HEAD_DIM:]
    visible = jnp.broadcast_to((flags_in > 0)[None, :], (half_rows, flags_in.shape[0]))
    after_prefix = (
        advance(begun[0], lower_queries, key_rows, value_rows, visible),
        advance(begun[1], upper_queries, key_rows, value_rows, visible),
    )
    slot_count = 4 * (row_count // BLK)
    empty_cache = jnp.zeros((slot_count * BLK, head_count, 2 * HEAD_DIM), jnp.bfloat16)
    pairs_in = lax.all_gather(new_pairs, "ctx", axis=0, tiled=True)
    start_row = jnp.int32(0)
    key_rows = pairs_in[..., :HEAD_DIM]
    value_rows = pairs_in[..., HEAD_DIM:]
    key_pos = jnp.arange(pairs_in.shape[0], dtype=jnp.int32)

    def update(states_now, query_set, query_pos):

        def compute(inner_state):
            return advance(
                inner_state, query_set, key_rows, value_rows, key_pos[None, :] <= query_pos[:, None]
            )

        def unchanged(inner_state):
            return inner_state

        return lax.cond(start_row <= query_pos[-1], compute, unchanged, states_now)

    lower_state = update(after_prefix[0], lower_queries, lower_pos)
    upper_state = update(after_prefix[1], upper_queries, upper_pos)
    pairs_in = lax.all_gather(new_pairs, "ctx", axis=0, tiled=True)
    block_count = pairs_in.shape[0] // BLK
    slot_blocks = (
        lax.all_gather(targets, "ctx", axis=0, tiled=True).reshape(block_count, BLK)[:, 0]
        - device * slot_count
    )
    onehot = (slot_blocks[None, :] == jnp.arange(slot_count, dtype=jnp.int32)[:, None]).astype(
        jnp.bfloat16
    )
    placed_rows = jnp.dot(
        onehot, pairs_in.reshape(block_count, -1), preferred_element_type=jnp.float32
    ).astype(jnp.bfloat16)
    decode_rows = placed_rows.reshape(empty_cache.shape)
    lower_out = finish(lower_state)
    upper_out = finish(upper_state)
    return (jnp.concatenate([lower_out, upper_out], 0), decode_rows)


def solution(mesh):
    placed = (
        P(("groups", "ctx"), ("head", "section")),
        P(),
        P("ctx", ("head", "section")),
        P(("groups", "ctx"), ("head", "section"), None),
        P(("groups", "ctx")),
        P("groups"),
        P(("groups", "ctx")),
    )
    return jax.shard_map(
        local,
        mesh=mesh,
        in_specs=placed,
        out_specs=(
            P(("groups", "ctx"), ("head", "section")),
            P(("groups", "ctx"), ("head", "section"), None),
        ),
        check_vma=False,
    )
```

profile of v0, /device:TPU:0, one launch (start us, length us, event | category | flops | bytes accessed | tf_op | source)
XLA Modules:
  0.0 836.1 jit_solution(12816791012417678506)
XLA Ops:
  12.2 13.5 %all-gather = s32[4,1,512]{2,1,0:T(1,128)S(1)} all-gather(s32[1,1,512]{2,1,0:T(1,128)S(1)} %bitcast.159), channel_id=1, replica_groups=mesh['groups'=2,'ctx'=4,'head'=2,'section'=2] {'ctx'}, dimensions={0}, use_global_device_ids=true | all-gather | bytes 10240 | tf_op jit(solution)/shard_map/all_gather | solution.py:98
  29.0 9.6 %all-gather.1 = s32[4,1,128]{2,1,0:T(1,128)S(1)} all-gather(s32[1,1,128]{2,1,0:T(1,128)S(1)} %broadcast.206), channel_id=1, replica_groups=mesh['groups'=2,'ctx'=4,'head'=2,'section'=2] {'ctx'}, dimensions={0}, use_global_device_ids=true | all-gather | bytes 2560 | tf_op jit(solution)/shard_map/all_gather | solution.py:131
  39.3 2.1 fusion.32
  41.4 694.9 %all-gather.8.cloned.1.call-done = bf16[8192,2560]{1,0:T(8,128)(2,1)} async-done(((bf16[2048,2560]{1,0:T(8,128)(2,1)}), bf16[8192,2560]{1,0:T(8,128)(2,1)}) %all-gather.8.cloned.1.call-update) | async-done | bytes 41943056 | tf_op jit(solution)/shard_map/all_gather | solution.py:77
  736.3 21.5 %fusion.41 = f32[128,2560]{0,1:T(8,128)S(1)} fusion(bf16[8192,2560]{1,0:T(8,128)(2,1)} %all-gather.8.cloned.1.call-done, bf16[128,8192]{1,0:T(8,128)(2,1)} %all-gather.6.cloned.1.call-done, f32[8192]{0:T(1024)S(1)} %convert_element_type.69, f32[128]{0:T(128)S(1)} %add_rsqrt_fusion), kind=kOutput, calls=%fused_computation.58 | convolution fusion | flops 5372903424 | bytes 45384192 | tf_op jit(solution)/shard_map/dot_general | solution.py:76
  758.4 1.3 copy.158
  759.8 26.1 %all_gather.23 = bf16[512,2,256]{0,2,1:T(8,128)(2,1)S(1)} all-gather(bf16[128,2,256]{0,2,1:T(8,128)(2,1)S(1)} %pad_maximum_fusion.2), channel_id=1, replica_groups=mesh['groups'=2,'ctx'=4,'head'=2,'section'=2] {'ctx'}, dimensions={0}, use_global_device_ids=true | all-gather | bytes 655360 | tf_op jit(solution)/shard_map/all_gather | solution.py:108
  787.0 1.5 subtract_convert_fusion
  789.5 1.4 all-gather.10.cloned.1.call-done
  790.9 2.9 fusion.25
  793.8 3.2 fusion.29
  797.1 2.0 fusion.31
  801.0 2.5 fusion.54
  803.4 7.1 conditional.2
  804.2 2.0 fusion.4
  807.9 2.6 fusion.5
  810.6 1.3 divide_convert_fusion.1
  812.7 6.1 fusion.51
  818.8 5.3 conditional.3
  819.8 1.4 fusion.15
  821.5 2.6 fusion.16
  824.2 1.3 divide_convert_fusion
  825.6 1.4 reshape.233
  827.4 1.3 reshape.234
  (92 shorter events, 15.8 us)
Async XLA Ops:
  7.2 32.1 %all-gather.6.cloned.1.call-start = ((), (), s32[]{:S(2)}) async-start(), calls=%async_computation | async-start | bytes 2621440 | tf_op jit(solution)/shard_map/all_gather | solution.py:71
  7.9 1.0 copy-start.7
  7.9 1.9 copy-start.12
  7.9 728.4 %all-gather.8.cloned.1.call-start = ((), (), s32[]{:S(2)}) async-start(), calls=%async_computation.1 | async-start | bytes 52428800 | tf_op jit(solution)/shard_map/all_gather | solution.py:77
  8.7 782.3 %all-gather.10.cloned.1.call-start = ((), (), s32[]{:S(2)}) async-start(), calls=%async_computation.2 | async-start | bytes 2621440 | tf_op jit(solution)/shard_map/all_gather | solution.py:97
  25.8 775.1 %copy-start.11 = (pred[1,4,4,128]{3,1,2,0:T(4,128)(4,1)}, pred[1,4,4,128]{3,1,2,0:T(4,128)(4,1)S(1)}, u32[]{:S(2)}) copy-start(pred[1,4,4,128]{3,1,2,0:T(4,128)(4,1)S(1)} %copy.160) | copy-start | bytes 6148
  27.1 1.9 copy-start.14
  758.4 28.6 %copy-start.10 = (f32[128,64]{1,0:T(8,128)S(1)}, f32[128,64]{1,0:T(8,128)}, u32[]{:S(2)}) copy-start(f32[128,64]{1,0:T(8,128)} %copy.118) | copy-start | bytes 98308
  789.5 13.9 %copy-start.1 = (bf16[512,2,128]{0,2,1:T(8,128)(2,1)}, bf16[512,2,128]{0,2,1:T(8,128)(2,1)S(1)}, u32[]{:S(2)}) copy-start(bf16[512,2,128]{0,2,1:T(8,128)(2,1)S(1)} %get-tuple-element.181) | copy-start | bytes 786436
  790.9 2.9 copy-start.6
  797.1 3.2 copy-start
  803.4 0.7 copy-start.5
  803.5 0.6 copy-start.8
  812.7 6.1 copy-start.2
  812.7 6.1 copy-start.4
  812.7 6.1 copy-start.15
  818.8 8.2 copy-start.13
  819.2 0.6 copy-start.9
  824.2 4.6 copy-start.3
Sparse Core Ops, SparseCore 0:
  9.6 25.2 all-gather.5
  36.5 699.7 all-gather.7
  738.4 52.4 all-gather.9
where the time goes:
time: 837 us; the launch traced here: 836 us
  waiting for transfers between devices  698 us (83%)
  blocking collectives  49.3 us (6%)
  matrix products  42.9 us (5%)
  between operations  17.4 us (2%)
  other arithmetic  15.9 us (2%)
  local copies, waits for them, and re-layouts  12.5 us (1%)
    all_gather x1, waiting for transfers between devices, local(): lax.all_gather(w_qkv, 'ctx', axis=0, tiled=True)  695 us
    all_gather x1, blocking collectives, local(): pairs_in = lax.all_gather(new_pairs, 'ctx', axis=0, tiled=True)  26.1 us
    dot_general x1, matrix products, local(): jnp.dot(normed, lax.all_gather(w_qkv, 'ctx', axis=0, tiled=True), preferr...  21.5 us
  transfers between devices with their start and end apart: 3, of which 2 were waited for; matrix products, arithmetic and copies ran while one was open for 4% of the time, Pallas kernels for 0%

commit v1 on v0

--- a/solution.py
+++ b/solution.py
@@ -68,14 +68,17 @@
 def local(tokens, norm_gain, w_qkv, prefix_kv, prefix_counts, span_offset, handoff_slots):
     row_count = tokens.shape[0]
     device = lax.axis_index("ctx")
-    features = lax.all_gather(tokens, ("head", "section"), axis=1, tiled=True)
-    values = features.astype(jnp.float32)
-    scale_row = lax.rsqrt(jnp.mean(values * values, -1, keepdims=True) + NORM_EPS)
-    normed = (values * scale_row * norm_gain.astype(jnp.float32)).astype(jnp.bfloat16)
+    values = tokens.astype(jnp.float32)
+    square_sum = lax.psum(jnp.sum(values * values, -1, keepdims=True), ("head", "section"))
+    scale_row = lax.rsqrt(square_sum / norm_gain.shape[0] + NORM_EPS)
+    hs = lax.axis_index("head") * lax.axis_size("section") + lax.axis_index("section")
+    gain = lax.dynamic_slice_in_dim(norm_gain, hs * tokens.shape[1], tokens.shape[1], 0)
+    normed = (values * scale_row * gain.astype(jnp.float32)).astype(jnp.bfloat16)
+    normed = lax.all_gather(normed, ("head", "section"), axis=1, tiled=True)
+    normed = lax.all_to_all(normed, "ctx", split_axis=1, concat_axis=0, tiled=True)
     proj_width = w_qkv.shape[1]
-    projected = jnp.dot(
-        normed, lax.all_gather(w_qkv, "ctx", axis=0, tiled=True), preferred_element_type=jnp.float32
-    )
+    partial = jnp.dot(normed, w_qkv, preferred_element_type=jnp.float32)
+    projected = lax.psum_scatter(partial, "ctx", scatter_dimension=0, tiled=True)
     head_count = proj_width // ((GROUP + 2) * HEAD_DIM)
     projected = projected.reshape(row_count, head_count, GROUP + 2, HEAD_DIM)
     local_pos = device * row_count + jnp.arange(row_count, dtype=jnp.int32)

time: 837 us -> 280 us (0.33)
  waiting for transfers between devices: 698 us -> 111 us
  blocking collectives: 49.3 us -> 99.7 us
  matrix products: 42.9 us -> 25.9 us
    all_gather x2 -> x1, waiting for transfers between devices: 695 us -> 23 us  [local(): normed = lax.all_gather(normed, ('head', 'section'), axis=1, tiled=True)]
    reduce_scatter x0 -> x1, waiting for transfers between devices: none -> 64.7 us  [local(): lax.psum_scatter(partial, 'ctx', scatter_dimension=0, tiled=True)]
    all_to_all x0 -> x1, blocking collectives: none -> 53.2 us  [local(): lax.all_to_all(normed, 'ctx', split_axis=1, concat_axis=0, tiled=True)]
    all_gather x1, waiting for transfers between devices: 1.39 us -> 23.3 us  [local(): pairs_in = lax.all_gather(prefix_kv, 'ctx', axis=0, tiled=True)]
    dot_general x1, matrix products: 21.5 us -> 10.4 us  [local(): partial = jnp.dot(normed, w_qkv, preferred_element_type=jnp.float32)]
    all_gather x1, blocking collectives: 26.1 us -> 17.6 us  [local(): pairs_in = lax.all_gather(new_pairs, 'ctx', axis=0, tiled=True)]
  transfers between devices with their start and end apart: 3 -> 3, of which waited for: 2 -> 3; matrix products, arithmetic and copies ran while one was open for 4% -> 4% of each run, Pallas kernels for 0% -> 0%
where the time goes in v1:
time: 280 us; the launch traced here: 279 us
  waiting for transfers between devices  111 us (40%)
  blocking collectives  99.7 us (36%)
  matrix products  25.9 us (9%)
  between operations  17.3 us (6%)
  local copies, waits for them, and re-layouts  15.6 us (6%)
  other arithmetic  9.21 us (3%)
    reduce_scatter x1, waiting for transfers between devices, local(): lax.psum_scatter(partial, 'ctx', scatter_dimension=0, tiled=True)  64.7 us
    all_to_all x1, blocking collectives, local(): lax.all_to_all(normed, 'ctx', split_axis=1, concat_axis=0, tiled=True)  53.2 us
    all_gather x1, waiting for transfers between devices, local(): pairs_in = lax.all_gather(prefix_kv, 'ctx', axis=0, tiled=True)  23.3 us
    all_gather x1, waiting for transfers between devices, local(): normed = lax.all_gather(normed, ('head', 'section'), axis=1, tiled=True)  23 us
    all_gather x1, blocking collectives, local(): pairs_in = lax.all_gather(new_pairs, 'ctx', axis=0, tiled=True)  17.6 us
    all_gather x1, blocking collectives, local(): flags_in = lax.all_gather(live_rows, 'ctx', axis=0, tiled=True)  12 us
    dot_general x1, matrix products, local(): partial = jnp.dot(normed, w_qkv, preferred_element_type=jnp.float32)  10.4 us
    all_gather x1, blocking collectives, local(): lax.all_gather(targets, 'ctx', axis=0, tiled=True).reshape(block_count, BLK)  8.53 us
  transfers between devices with their start and end apart: 3, of which 3 were waited for; matrix products, arithmetic and copies ran while one was open for 4% of the time, Pallas kernels for 0%

profile of v1, /device:TPU:0, one launch (start us, length us, event | category | flops | bytes accessed | tf_op | source)
XLA Modules:
  0.0 279.2 jit_solution(12474117400058852650)
XLA Ops:
  7.2 1.3 copy.146
  8.8 8.3 %psum.7 = f32[128,1]{0,1:T(1,128)S(1)} all-reduce(f32[128,1]{0,1:T(1,128)S(1)} %bitcast.172), channel_id=1, replica_groups=mesh['groups'=2,'ctx'=4,'head'=2,'section'=2] {'head','section'}, use_global_device_ids=true, to_apply=%region_1.0 | all-reduce | flops 128 | bytes 1024 | tf_op jit(solution)/shard_map/psum | solution.py:72
  17.9 1.1 fusion.52
  19.1 23.0 %all-gather.5.cloned.1.call-done = bf16[128,8192]{0,1:T(8,128)(2,1)} async-done(((bf16[128,2048]{0,1:T(8,128)(2,1)}), bf16[128,8192]{0,1:T(8,128)(2,1)}) %all-gather.5.cloned.1.call-update) | async-done | bytes 2097168 | tf_op jit(solution)/shard_map/all_gather | solution.py:77
  42.1 53.2 %all_to_all.19 = bf16[128,4,2048]{0,2,1:T(8,128)(2,1)S(1)} all-to-all(bf16[128,4,2048]{0,2,1:T(8,128)(2,1)} %bitcast.158), channel_id=1, replica_groups=mesh['groups'=2,'ctx'=4,'head'=2,'section'=2] {'ctx'}, dimensions={1} | all-to-all | bytes 4194304 | tf_op jit(solution)/shard_map/all_to_all | solution.py:78
  95.3 2.7 copy.147
  98.0 10.4 %fusion.70 = f32[512,2560]{1,0:T(8,128)} fusion(bf16[512,2048]{1,0:T(8,128)(2,1)} %bitcast.159, bf16[2048,2560]{1,0:T(8,128)(2,1)} %param.13), kind=kOutput, calls=%fused_computation.114 | convolution fusion | flops 5368709120 | bytes 17825792 | tf_op jit(solution)/shard_map/dot_general | solution.py:80
  114.8 12.0 %all-gather = s32[4,1,512]{2,1,0:T(1,128)S(1)} all-gather(s32[1,1,512]{2,1,0:T(1,128)S(1)} %bitcast.169), channel_id=1, replica_groups=mesh['groups'=2,'ctx'=4,'head'=2,'section'=2] {'ctx'}, dimensions={0}, use_global_device_ids=true | all-gather | bytes 10240 | tf_op jit(solution)/shard_map/all_gather | solution.py:101
  127.3 8.5 %all-gather.1 = s32[4,1,128]{2,1,0:T(1,128)S(1)} all-gather(s32[1,1,128]{2,1,0:T(1,128)S(1)} %broadcast.196), channel_id=1, replica_groups=mesh['groups'=2,'ctx'=4,'head'=2,'section'=2] {'ctx'}, dimensions={0}, use_global_device_ids=true | all-gather | bytes 2560 | tf_op jit(solution)/shard_map/all_gather | solution.py:134
  136.0 64.7 %reduce-scatter.2.cloned.1.call-done = f32[128,2560]{1,0:T(8,128)} async-done(((f32[512,2560]{1,0:T(8,128)}), f32[128,2560]{1,0:T(8,128)}) %reduce-scatter.2.cloned.1.call-update) | async-done | bytes 1310736 | tf_op jit(solution)/shard_map/reduce_scatter | solution.py:81
  200.7 1.7 copy.148
  202.5 17.6 %all_gather.19 = bf16[512,2,256]{0,2,1:T(8,128)(2,1)S(1)} all-gather(bf16[128,2,256]{0,2,1:T(8,128)(2,1)S(1)} %pad_maximum_fusion.2), channel_id=1, replica_groups=mesh['groups'=2,'ctx'=4,'head'=2,'section'=2] {'ctx'}, dimensions={0}, use_global_device_ids=true | all-gather | bytes 655360 | tf_op jit(solution)/shard_map/all_gather | solution.py:111
  221.3 1.3 reshape.229
  223.5 1.4 copy.191
  224.9 1.3 copy.190
  226.3 1.5 subtract_convert_fusion
  228.1 23.3 %all-gather.7.cloned.1.call-done = bf16[2048,2,256]{2,0,1:T(8,128)(2,1)} async-done(((bf16[512,2,256]{2,0,1:T(8,128)(2,1)}), bf16[2048,2,256]{2,0,1:T(8,128)(2,1)}) %all-gather.7.cloned.1.call-update) | async-done | bytes 2097168 | tf_op jit(solution)/shard_map/all_gather | solution.py:100
  251.4 2.9 %fusion.25 = (f32[64,2,8]{2,0,1:T(8,128)S(1)}, f32[2,64,8,2048]{3,2,1,0:T(8,128)S(1)}) fusion(pred[2048]{0:T(1024)(128)(4,1)S(1)} %bitcast.164, bf16[2048,2,256]{2,0,1:T(8,128)(2,1)} %all-gather.7.cloned.1.call-done, bf16[128,2,8,64]{3,2,0,1:T(8,128)(2,1)S(1)} %get-tuple-element.191, bf16[128,2,8,64]{3,2,0,1:T(8,128)(2,1)S(1)} %get-tuple-element.190), kind=kOutput, calls=%fused_computation.42 | convolution fusion | flops 544209920 | bytes 9967616 | tf_op jit(solution)/shard_map/rhgd,khd->rhgk/dot_general | solution.py:45
  254.3 3.2 %fusion.29 = (f32[64,2,8]{2,0,1:T(8,128)S(1)}, f32[64,2,8]{2,0,1:T(8,128)S(1)}, f32[2,64,8,2048]{3,2,1,0:T(8,128)S(1)}) fusion(f32[2,64,8,2048]{3,2,1,0:T(8,128)S(1)} %get-tuple-element.207, f32[64,2,8]{2,0,1:T(8,128)S(1)} %broadcast_maximum_fusion.1, pred[2048]{0:T(1024)(128)(4,1)S(1)} %bitcast.165, bf16[2048,2,256]{2,0,1:T(8,128)(2,1)S(1)} %copy-done.1, ...), kind=kOutput, calls=%fused_computation.46 | convolution fusion | flops 552597504 | bytes 18950144 | tf_op jit(solution)/shard_map/rhgd,khd->rhgk/dot_general | solution.py:45
  257.6 2.0 fusion.31
  259.6 1.7 fusion.44
  261.2 2.7 conditional.3
  264.3 4.7 %fusion.47 = f32[64,2,8,128]{3,2,0,1:T(8,128)S(1)} fusion(f32[2,64,8,2048]{3,2,1,0:T(8,128)} %copy-done, f32[64,2,8]{2,0,1:T(8,128)S(1)} %broadcast_maximum_fusion.1, pred[2048]{0:T(1024)(128)(4,1)S(1)} %bitcast.168, bf16[2048,2,256]{2,0,1:T(8,128)(2,1)} %all-gather.7.cloned.1.call-done, f32[64,2,8]{2,0,1:T(8,128)S(1)} %get-tuple-element.210), kind=kOutput, calls=%fused_computation.58 | convolution fusion | flops 545390592 | bytes 9971712 | tf_op jit(solution)/shard_map/rhgk,khd->rhgd/dot_general | solution.py:53
  269.0 2.5 conditional.2
  (72 shorter events, 13.5 us)
Async XLA Ops:
  7.2 34.9 %all-gather.5.cloned.1.call-start = ((), (), s32[]{:S(2)}) async-start(), calls=%async_computation.2 | async-start | bytes 2621440 | tf_op jit(solution)/shard_map/all_gather | solution.py:77
  19.0 181.7 %reduce-scatter.2.cloned.1.call-start = ((), (), s32[]{:S(2)}) async-start(), calls=%async_computation.3 | async-start | bytes 6553600 | tf_op jit(solution)/shard_map/reduce_scatter | solution.py:81
  108.4 1.0 copy-start.2
  108.4 142.9 %all-gather.7.cloned.1.call-start = ((), (), s32[]{:S(2)}) async-start(), calls=%async_computation.4 | async-start | bytes 2621440 | tf_op jit(solution)/shard_map/all_gather | solution.py:100
  251.4 2.9 %copy-start.1 = (bf16[2048,2,256]{2,0,1:T(8,128)(2,1)S(1)}, bf16[2048,2,256]{2,0,1:T(8,128)(2,1)}, u32[]{:S(2)}) copy-start(bf16[2048,2,256]{2,0,1:T(8,128)(2,1)} %all-gather.7.cloned.1.call-done) | copy-start | bytes 6291460
  254.3 3.3 %copy-start = (f32[2,64,8,2048]{3,2,1,0:T(8,128)}, f32[2,64,8,2048]{3,2,1,0:T(8,128)S(1)}, u32[]{:S(2)}) copy-start(f32[2,64,8,2048]{3,2,1,0:T(8,128)S(1)} %get-tuple-element.207) | copy-start | bytes 25165828
Sparse Core Ops, SparseCore 0:
  19.1 22.8 all-gather.4
  108.6 92.0 reduce-scatter.1
  202.8 48.5 all-gather.6

commit v2 on v0

v2 whole, which is shorter than its diff:
```python
import functools
import math

import jax
import jax.numpy as jnp
from jax import lax
from jax.experimental import pallas as pl
from jax.experimental.pallas import tpu as pltpu
from jax.sharding import PartitionSpec as P

HEAD_DIM = 128
GROUP = 8
BLK = 128
ROPE_BASE = 500000.0
NORM_EPS = 1e-05
CW = 640
MESH = pl.DeviceIdType.MESH


def kernel(
    n, nh, ns, wire,
    tok_ref, gain_ref, w_hbm, pre_hbm, meta_in, cos_ref, sin_ref,
    att_ref, dec_ref,
    ss, stage, xfull, w_ref, part, outb, recv, pre, newkv, meta, qbuf, sbuf,
    wsem, psem, ss_s, ss_r, st_s, x_s, x_r, rs_s, rs_r, pre_s, pre_r, new_s, new_r, meta_s, meta_r,
):
    c = lax.axis_index("ctx")
    h = lax.axis_index("head")
    s = lax.axis_index("section")
    nhs = nh * ns
    hs = h * ns + s
    r = n // nhs
    rows, width = tok_ref.shape
    fw = width // r
    heads = pre.shape[1]
    nch = part.shape[1]
    prow = pre.shape[2]
    f32 = jnp.float32

    def plane(offset):
        other = lax.rem(hs + offset, nhs)
        return {"head": other // ns, "section": lax.rem(other, ns)}

    def rcopy(src, dst, ssem, rsem, dev):
        return pltpu.make_async_remote_copy(
            src_ref=src, dst_ref=dst, send_sem=ssem, recv_sem=rsem,
            device_id=dev, device_id_type=MESH,
        )

    wcopy = pltpu.make_async_copy(w_hbm, w_ref, wsem)
    wcopy.start()
    pcopy = pltpu.make_async_copy(pre_hbm, pre.at[c], psem)
    pcopy.start()

    barrier = pltpu.get_barrier_semaphore()
    for o in range(1, n):
        pl.semaphore_signal(
            barrier, inc=1, device_id={"ctx": lax.rem(c + o, n)}, device_id_type=MESH
        )
    for o in range(1, nhs):
        pl.semaphore_signal(barrier, inc=1, device_id=plane(o), device_id_type=MESH)

    values = tok_ref[...].astype(f32)
    acc = jnp.zeros((rows, 128), f32)
    for j in range(width // 128):
        piece = values[:, j * 128:(j + 1) * 128]
        acc = acc + piece * piece
    ss[hs] = acc
    meta[c] = meta_in[...]
    pl.semaphore_wait(barrier, n - 1 + nhs - 1)

    def ss_copy(o):
        return rcopy(ss.at[hs], ss.at[hs], ss_s.at[o], ss_r.at[hs], plane(o))

    for o in range(1, nhs):
        ss_copy(o).start()

    def meta_copy(o):
        return rcopy(
            meta.at[c], meta.at[c], meta_s.at[o], meta_r.at[c], {"ctx": lax.rem(c + o, n)}
        )

    def pre_copy(o):
        return rcopy(
            pre.at[c], pre.at[c], pre_s.at[o], pre_r.at[c], {"ctx": lax.rem(c + o, n)}
        )

    def new_copy(o):
        return rcopy(
            newkv.at[c], newkv.at[c], new_s.at[o], new_r.at[c], {"ctx": lax.rem(c + o, n)}
        )

    for o in range(1, nhs):
        other = lax.rem(hs + o, nhs)
        rcopy(ss.at[other], ss.at[other], ss_s.at[o], ss_r.at[other], plane(o)).wait_recv()
    total_sq = ss[0]
    for i in range(1, nhs):
        total_sq = total_sq + ss[i]
    scale = lax.rsqrt(jnp.sum(total_sq, -1, keepdims=True) / (width * nhs) + NORM_EPS)
    gain = gain_ref[:, pl.ds(pl.multiple_of(hs * width, 128), width)]
    normed = (tok_ref[...].astype(f32) * scale * gain.astype(f32)).astype(jnp.bfloat16)

    def st_copy(j):
        return rcopy(stage.at[j], xfull.at[c], st_s.at[j], x_r.at[c], {"ctx": hs * r + j})

    for j in range(r):
        piece = normed[:, j * fw:(j + 1) * fw]

        @pl.when(hs * r + j == c)
        def _():
            xfull[c] = piece

        @pl.when(hs * r + j != c)
        def _():
            stage[j] = piece
            st_copy(j).start()

    for o in range(1, n):
        meta_copy(o).start()
    pcopy.wait()
    for o in range(1, n):
        pre_copy(o).start()

    root = c // r
    root_h = root // ns
    root_s = lax.rem(root, ns)
    is_root = hs == root

    def x_copy(d, o):
        dev = {"section": lax.rem(s + 1, ns)} if o == 0 else {"head": lax.rem(h + o, nh)}
        return rcopy(xfull.at[d], xfull.at[d], x_s.at[d, o], x_r.at[d], dev)

    def x_arrive(d):
        @pl.when(jnp.logical_or(jnp.logical_not(is_root), d != c))
        def _():
            x_copy(d, 0).wait_recv()

        @pl.when(s == root_s)
        def _():
            @pl.when(h == root_h)
            def _():
                for o in range(1, nh):
                    x_copy(d, o).start()

            x_copy(d, 0).start()

    def rs_copy(d, k, right):
        if right:
            return rcopy(
                outb.at[d, k], recv.at[d, k], rs_s.at[d, k], rs_r.at[d, k], {"ctx": c + 1}
            )
        slot = jnp.where(d == c - 1, n, d)
        return rcopy(
            outb.at[d, k], recv.at[slot, k], rs_s.at[d, k], rs_r.at[slot, k], {"ctx": c - 1}
        )

    def rs_arrive(slot, k):
        rcopy(
            outb.at[0, k], recv.at[slot, k], rs_s.at[0, k], rs_r.at[slot, k],
            {"ctx": lax.rem(c + 1, n)},
        ).wait_recv()

    def dot(d, k):
        return jnp.dot(
            xfull[d], w_ref[:, pl.ds(pl.multiple_of(k * CW, 128), CW)],
            preferred_element_type=f32,
        )

    wcopy.wait()

    def forward(d, right):
        @pl.loop(0, nch)
        def _(k):
            first = (c == 0) if right else (c == n - 1)

            @pl.when(first)
            def _():
                outb[d, k] = dot(d, k).astype(wire)

            @pl.when(jnp.logical_not(first))
            def _():
                own = dot(d, k)
                rs_arrive(d, k)
                outb[d, k] = (own + recv[d, k].astype(f32)).astype(wire)

            rs_copy(d, k, right).start()

    @pl.loop(0, n - 1)
    def _(t):
        @pl.when(n - 1 - t > c)
        def _():
            x_arrive(n - 1 - t)
            forward(n - 1 - t, True)

        @pl.when(t < c)
        def _():
            x_arrive(t)
            forward(t, False)

    x_arrive(c)

    @pl.loop(0, nch)
    def _(k):
        part[0, k] = dot(c, k)

    @pl.loop(0, nch)
    def _(k):
        @pl.when(c > 0)
        def _():
            rs_arrive(c, k)
            part[0, k] += recv[c, k].astype(f32)

        @pl.when(c < n - 1)
        def _():
            rs_arrive(n, k)
            part[0, k] += recv[n, k].astype(f32)

    cosines = cos_ref[...]
    sines = sin_ref[...]
    per = CW // HEAD_DIM

    def piece_of(g, j):
        i = g * (GROUP + 2) + j
        return part[0, i // per, :, (i % per) * HEAD_DIM:(i % per + 1) * HEAD_DIM]

    def turned(v):
        return v * cosines + pltpu.roll(v, HEAD_DIM // 2, 1) * sines

    for g in range(heads):
        newkv[c, g, :, :HEAD_DIM] = turned(piece_of(g, GROUP)).astype(jnp.bfloat16)
        newkv[c, g, :, HEAD_DIM:] = piece_of(g, GROUP + 1).astype(jnp.bfloat16)
    for o in range(1, n):
        new_copy(o).start()
    for g in range(heads):
        for j in range(GROUP):
            qbuf[g, j * rows:(j + 1) * rows] = turned(piece_of(g, j)).astype(jnp.bfloat16)

    for o in range(1, n):
        src = lax.rem(c + o, n)
        dev = {"ctx": src}
        rcopy(meta.at[src], meta.at[src], meta_s.at[o], meta_r.at[src], dev).wait_recv()
        rcopy(pre.at[src], pre.at[src], pre_s.at[o], pre_r.at[src], dev).wait_recv()
    for o in range(1, n):
        src = lax.rem(c + o, n)
        dev = {"ctx": src}
        rcopy(newkv.at[src], newkv.at[src], new_s.at[o], new_r.at[src], dev).wait_recv()

    tile = sbuf.shape[1]
    per_tile = tile // rows
    factor = 1.0 / math.sqrt(HEAD_DIM)
    nt = (((1,), (1,)), ((), ()))
    unroll = n <= 4

    @pl.loop(0, heads * GROUP // per_tile)
    def _(i):
        g = i // (GROUP // per_tile)
        jj = lax.rem(i, GROUP // per_tile)
        q = qbuf[g, pl.ds(pl.multiple_of(jj * tile, 128), tile)]

        def scores(b, top):
            sp = lax.dot_general(q, pre[b, g, :, :HEAD_DIM], nt, preferred_element_type=f32)
            count = meta[b, 0:1, :]
            for z in range(prow // BLK):
                piece = jnp.where(count > z, sp[:, z * BLK:(z + 1) * BLK] * factor, -1e30)
                sbuf[b, :, z * BLK:(z + 1) * BLK] = piece
                top = jnp.maximum(top, piece)
            sn = lax.dot_general(q, newkv[b, g, :, :HEAD_DIM], nt, preferred_element_type=f32)
            row = lax.broadcasted_iota(jnp.int32, (tile, BLK), 0) % rows + c * rows
            col = lax.broadcasted_iota(jnp.int32, (tile, BLK), 1) + b * BLK
            piece = jnp.where(col <= row, sn * factor, -1e30)
            sbuf[b, :, prow:] = piece
            return jnp.maximum(top, piece)

        top = lax.fori_loop(0, n, scores, jnp.full((tile, BLK), -1e30, f32), unroll=unroll)
        peak = jnp.max(top, -1, keepdims=True)

        def blend(b, state):
            lsum, acc = state
            w = jnp.exp(sbuf[b] - peak)
            for z in range(w.shape[1] // BLK):
                lsum = lsum + w[:, z * BLK:(z + 1) * BLK]
            wb = w.astype(jnp.bfloat16)
            acc = acc + jnp.dot(
                wb[:, :prow], pre[b, g, :, HEAD_DIM:], preferred_element_type=f32
            )
            acc = acc + jnp.dot(
                wb[:, prow:], newkv[b, g, :, HEAD_DIM:], preferred_element_type=f32
            )
            return lsum, acc

        lsum, acc = lax.fori_loop(
            0, n, blend,
            (jnp.zeros((tile, BLK), f32), jnp.zeros((tile, HEAD_DIM), f32)),
            unroll=unroll,
        )
        out = (acc / jnp.sum(lsum, -1, keepdims=True)).astype(jnp.bfloat16)
        for z in range(per_tile):
            col = pl.multiple_of((i * per_tile + z) * HEAD_DIM, 128)
            att_ref[:, pl.ds(col, HEAD_DIM)] = out[z * rows:(z + 1) * rows]

    slots = dec_ref.shape[1] // BLK
    for g in range(heads):
        for q in range(slots):
            def pick(b, now):
                hit = meta[b, 1:2, 0:1] == c * slots + q
                return jnp.where(hit, newkv[b, g].astype(f32), now)

            found = lax.fori_loop(
                0, n, pick, jnp.zeros((BLK, 2 * HEAD_DIM), f32), unroll=unroll
            )
            dec_ref[g, q * BLK:(q + 1) * BLK] = found.astype(jnp.bfloat16)

    for o in range(1, nhs):
        ss_copy(o).wait_send()
    for j in range(r):
        @pl.when(hs * r + j != c)
        def _():
            st_copy(j).wait_send()
    for o in range(1, n):
        meta_copy(o).wait_send()
        pre_copy(o).wait_send()
        new_copy(o).wait_send()

    @pl.when(s == root_s)
    def _():
        @pl.loop(0, n)
        def _(d):
            @pl.when(h == root_h)
            def _():
                for o in range(1, nh):
                    x_copy(d, o).wait_send()

            x_copy(d, 0).wait_send()

    @pl.loop(0, n)
    def _(d):
        @pl.loop(0, nch)
        def _(k):
            @pl.when(d > c)
            def _():
                rs_copy(d, k, True).wait_send()

            @pl.when(d < c)
            def _():
                rs_copy(d, k, False).wait_send()


def local(n, nh, ns, tokens, norm_gain, w_qkv, prefix_kv, prefix_counts, span_offset, handoff_slots):
    rows, width = tokens.shape
    heads = prefix_kv.shape[1]
    prow = prefix_kv.shape[0]
    nch = w_qkv.shape[1] // CW
    fw = w_qkv.shape[0]
    slots = prow // BLK
    c = lax.axis_index("ctx")
    half = HEAD_DIM // 2
    frequency = ROPE_BASE ** (-(jnp.arange(half, dtype=jnp.float32) * 2.0) / HEAD_DIM)
    positions = (
        span_offset[0] * BLK + c * rows + jnp.arange(rows, dtype=jnp.int32)
    ).astype(jnp.float32)
    angles = positions[:, None] * frequency[None, :]
    cosines = jnp.cos(angles)
    sines = jnp.sin(angles)
    cosines = jnp.concatenate([cosines, cosines], -1)
    sines = jnp.concatenate([-sines, sines], -1)
    meta = jnp.concatenate([
        jnp.broadcast_to(prefix_counts[:, None], (1, 128)),
        jnp.broadcast_to(handoff_slots[:, None], (7, 128)),
    ], 0)
    wire = jnp.float32
    bf16 = jnp.bfloat16
    nhs = nh * ns
    vmem = pl.BlockSpec(memory_space=pltpu.VMEM)
    hbm = pl.BlockSpec(memory_space=pl.ANY)
    tile = 256 if n <= 4 else 128
    dma = pltpu.SemaphoreType.DMA
    att, dec = pl.pallas_call(
        functools.partial(kernel, n, nh, ns, wire),
        out_shape=(
            jax.ShapeDtypeStruct((rows, heads * GROUP * HEAD_DIM), bf16),
            jax.ShapeDtypeStruct((heads, slots * BLK, 2 * HEAD_DIM), bf16),
        ),
        in_specs=[vmem, vmem, hbm, hbm, vmem, vmem, vmem],
        out_specs=(vmem, vmem),
        scratch_shapes=[
            pltpu.VMEM((nhs, rows, 128), jnp.float32),
            pltpu.VMEM((n // nhs, rows, fw), bf16),
            pltpu.VMEM((n, rows, fw), bf16),
            pltpu.VMEM(w_qkv.shape, bf16),
            pltpu.VMEM((1, nch, rows, CW), jnp.float32),
            pltpu.VMEM((n, nch, rows, CW), wire),
            pltpu.VMEM((n + 1, nch, rows, CW), wire),
            pltpu.VMEM((n, heads, prow, 2 * HEAD_DIM), bf16),
            pltpu.VMEM((n, heads, rows, 2 * HEAD_DIM), bf16),
            pltpu.VMEM((n, 8, 128), jnp.int32),
            pltpu.VMEM((heads, GROUP * rows, HEAD_DIM), bf16),
            pltpu.VMEM((n, tile, prow + rows), jnp.float32),
            dma, dma,
            dma((nhs,)), dma((nhs,)),
            dma((n // nhs,)),
            dma((n, nh)), dma((n,)),
            dma((n, nch)), dma((n + 1, nch)),
            dma((n,)), dma((n,)), dma((n,)), dma((n,)), dma((n,)), dma((n,)),
        ],
        compiler_params=pltpu.CompilerParams(
            collective_id=0, has_side_effects=True, vmem_limit_bytes=56 * 1024 * 1024
        ),
    )(
        tokens, norm_gain.reshape(1, -1), w_qkv, prefix_kv.transpose(1, 0, 2), meta,
        cosines, sines,
    )
    return att, dec.transpose(1, 0, 2)


def solution(mesh):
    placed = (
        P(("groups", "ctx"), ("head", "section")),
        P(),
        P("ctx", ("head", "section")),
        P(("groups", "ctx"), ("head", "section"), None),
        P(("groups", "ctx")),
        P("groups"),
        P(("groups", "ctx")),
    )
    return jax.shard_map(
        functools.partial(
            local, mesh.shape["ctx"], mesh.shape["head"], mesh.shape["section"]
        ),
        mesh=mesh,
        in_specs=placed,
        out_specs=(
            P(("groups", "ctx"), ("head", "section")),
            P(("groups", "ctx"), ("head", "section"), None),
        ),
        check_vma=False,
    )
```

time: 837 us -> 225 us (0.27)
  waiting for transfers between devices: 698 us -> 0 us
  Pallas kernels: 0 us -> 213 us
  blocking collectives: 49.3 us -> 0 us
  matrix products: 42.9 us -> 0 us
  other arithmetic: 15.9 us -> 1.07 us
  between operations: 17.4 us -> 2.61 us
    all_gather x3 -> x0, waiting for transfers between devices: 696 us -> none  [the longest x1 695 us: local(): lax.all_gather(w_qkv, 'ctx', axis=0, tiled=True)]
    pallas_call x0 -> x1, Pallas kernels: none -> 213 us  [local(): pl.pallas_call(functools.partial(kernel, n, nh, ns, wire), out_shape=(jax...]
    all_gather x3 -> x0, blocking collectives: 49.3 us -> none  [the longest x1 26.1 us: local(): pairs_in = lax.all_gather(new_pairs, 'ctx', axis=0, tiled=True)]
    dot_general x10 -> x0, matrix products: 42.9 us -> none  [the longest x1 21.5 us: local(): jnp.dot(normed, lax.all_gather(w_qkv, 'ctx', axis=0, tiled=True), preferr...]
  transfers between devices with their start and end apart: 3 -> 0, of which waited for: 2 -> 0; matrix products, arithmetic and copies ran while one was open for 4% -> 0% of each run, Pallas kernels for 0% -> 0%
where the time goes in v2:
time: 225 us
  Pallas kernels  213 us (95%)
  local copies, waits for them, and re-layouts  8.17 us (4%)
  between operations  2.61 us (1%)
    pallas_call x1, Pallas kernels, local(): pl.pallas_call(functools.partial(kernel, n, nh, ns, wire), out_shape=(jax...  213 us
    unnamed x3, local copies, waits for them, and re-layouts  6.16 us

profile of v2, /device:TPU:0, one launch (start us, length us, event | category | flops | bytes accessed | tf_op | source)
XLA Modules:
  0.0 224.6 jit_solution(4664278636929581631)
XLA Ops:
  2.6 0.7 concatenate.12.meta_in
  3.3 1.4 reshape.25.gain_ref
  4.6 0.3 fusion
  4.9 0.7 pad_maximum_fusion
  5.7 1.9 copy.12
  7.6 212.7 %shard_map.86 = (bf16[128,2048]{1,0:T(8,128)(2,1)}, bf16[2,512,256]{2,1,0:T(8,128)(2,1)}) custom-call(bf16[128,2048]{1,0:T(8,128)(2,1)} %tok_ref.1, bf16[1,8192]{1,0:T(2,128)(2,1)} %reshape.25.gain_ref, bf16[2048,2560]{1,0:T(8,128)(2,1)} %w_hbm.1, bf16[2,512,256]{2,1,0:T(8,128)(2,1)} %bitcast.8, s32[8,128]{1,0:T(8,128)} %concatenate.12.meta_in, ...), custom_call_target="tpu_custom_call" | custom-call | tf_op jit(solution)/shard_map/pallas_call | solution.py:377
  220.3 2.4 %copy.10 = bf16[512,2,256]{2,1,0:T(2,128)(2,1)} copy(bf16[512,2,256]{2,0,1:T(8,128)(2,1)} %bitcast.9) | data formatting | bytes 1048576
  222.7 1.9 copy.17
  (3 shorter events, 0.0 us)

commit v3 on v2

--- a/solution.py
+++ b/solution.py
@@ -53,12 +53,18 @@
     pcopy.start()
 
     barrier = pltpu.get_barrier_semaphore()
-    for o in range(1, n):
+    for o in range(1, n * nh):
+        other = lax.rem(c * nh + h + o, n * nh)
         pl.semaphore_signal(
-            barrier, inc=1, device_id={"ctx": lax.rem(c + o, n)}, device_id_type=MESH
-        )
-    for o in range(1, nhs):
-        pl.semaphore_signal(barrier, inc=1, device_id=plane(o), device_id_type=MESH)
+            barrier, inc=1, device_id={"ctx": other // nh, "head": lax.rem(other, nh)},
+            device_id_type=MESH,
+        )
+    for o in range(1, ns):
+        for p in range(nh):
+            pl.semaphore_signal(
+                barrier, inc=1, device_id={"head": p, "section": lax.rem(s + o, ns)},
+                device_id_type=MESH,
+            )
 
     values = tok_ref[...].astype(f32)
     acc = jnp.zeros((rows, 128), f32)
@@ -67,7 +73,7 @@
         acc = acc + piece * piece
     ss[hs] = acc
     meta[c] = meta_in[...]
-    pl.semaphore_wait(barrier, n - 1 + nhs - 1)
+    pl.semaphore_wait(barrier, n * nh - 1 + (ns - 1) * nh)
 
     def ss_copy(o):
         return rcopy(ss.at[hs], ss.at[hs], ss_s.at[o], ss_r.at[hs], plane(o))
@@ -80,14 +86,30 @@
             meta.at[c], meta.at[c], meta_s.at[o], meta_r.at[c], {"ctx": lax.rem(c + o, n)}
         )
 
-    def pre_copy(o):
+    def pre_copy(b, right):
+        dev = {"ctx": c + 1} if right else {"ctx": c - 1}
+        return rcopy(pre.at[b], pre.at[b], pre_s.at[int(right), b], pre_r.at[b], dev)
+
+    def pre_send(b, right):
+        @pl.when((c < n - 1) if right else (c > 0))
+        def _():
+            pre_copy(b, right).start()
+
+    def pre_step(t):
+        @pl.when(c - 1 - t >= 0)
+        def _():
+            pre_copy(c - 1 - t, False).wait_recv()
+            pre_send(c - 1 - t, True)
+
+        @pl.when(c + 1 + t <= n - 1)
+        def _():
+            pre_copy(c + 1 + t, True).wait_recv()
+            pre_send(c + 1 + t, False)
+
+    def new_copy(o, g):
         return rcopy(
-            pre.at[c], pre.at[c], pre_s.at[o], pre_r.at[c], {"ctx": lax.rem(c + o, n)}
-        )
-
-    def new_copy(o):
-        return rcopy(
-            newkv.at[c], newkv.at[c], new_s.at[o], new_r.at[c], {"ctx": lax.rem(c + o, n)}
+            newkv.at[c, g], newkv.at[c, g], new_s.at[o, g], new_r.at[c, g],
+            {"ctx": lax.rem(c + o, n)},
         )
 
     for o in range(1, nhs):
@@ -100,49 +122,61 @@
     gain = gain_ref[:, pl.ds(pl.multiple_of(hs * width, 128), width)]
     normed = (tok_ref[...].astype(f32) * scale * gain.astype(f32)).astype(jnp.bfloat16)
 
-    def st_copy(j):
-        return rcopy(stage.at[j], xfull.at[c], st_s.at[j], x_r.at[c], {"ctx": hs * r + j})
-
+    def st_copy(j, p):
+        return rcopy(
+            stage.at[j, p], xfull.at[c, p], st_s.at[j, p], x_r.at[c, p],
+            {"ctx": hs * r + j, "head": p},
+        )
+
+    def here(j, p):
+        return jnp.logical_and(hs * r + j == c, h == p)
+
+    prt = rows // nh
     for j in range(r):
-        piece = normed[:, j * fw:(j + 1) * fw]
-
-        @pl.when(hs * r + j == c)
-        def _():
-            xfull[c] = piece
-
-        @pl.when(hs * r + j != c)
-        def _():
-            stage[j] = piece
-            st_copy(j).start()
+        for p in range(nh):
+            piece = normed[p * prt:(p + 1) * prt, j * fw:(j + 1) * fw]
+
+            @pl.when(here(j, p))
+            def _():
+                xfull[c, p] = piece
+
+            @pl.when(jnp.logical_not(here(j, p)))
+            def _():
+                stage[j, p] = piece
+                st_copy(j, p).start()
 
     for o in range(1, n):
         meta_copy(o).start()
     pcopy.wait()
-    for o in range(1, n):
-        pre_copy(o).start()
+    pre_send(c, True)
+    pre_send(c, False)
 
     root = c // r
-    root_h = root // ns
     root_s = lax.rem(root, ns)
     is_root = hs == root
 
-    def x_copy(d, o):
+    def x_copy(d, p, o):
         dev = {"section": lax.rem(s + 1, ns)} if o == 0 else {"head": lax.rem(h + o, nh)}
-        return rcopy(xfull.at[d], xfull.at[d], x_s.at[d, o], x_r.at[d], dev)
+        return rcopy(xfull.at[d, p], xfull.at[d, p], x_s.at[d, p, o], x_r.at[d, p], dev)
 
     def x_arrive(d):
-        @pl.when(jnp.logical_or(jnp.logical_not(is_root), d != c))
-        def _():
-            x_copy(d, 0).wait_recv()
+        @pl.when(jnp.logical_not(jnp.logical_and(is_root, d == c)))
+        def _():
+            x_copy(d, h, 0).wait_recv()
 
         @pl.when(s == root_s)
         def _():
-            @pl.when(h == root_h)
-            def _():
-                for o in range(1, nh):
-                    x_copy(d, o).start()
-
-            x_copy(d, 0).start()
+            for o in range(1, nh):
+                x_copy(d, h, o).start()
+            x_copy(d, h, 0).start()
+
+        for o in range(1, nh):
+            p = lax.rem(h + o, nh)
+            x_copy(d, p, 0).wait_recv()
+
+            @pl.when(s == root_s)
+            def _():
+                x_copy(d, p, 0).start()
 
     def rs_copy(d, k, right):
         if right:
@@ -162,14 +196,16 @@
 
     def dot(d, k):
         return jnp.dot(
-            xfull[d], w_ref[:, pl.ds(pl.multiple_of(k * CW, 128), CW)],
+            xfull[d].reshape(rows, fw), w_ref[:, pl.ds(pl.multiple_of(k * CW, 128), CW)],
             preferred_element_type=f32,
         )
 
     wcopy.wait()
 
-    def forward(d, right):
-        @pl.loop(0, nch)
+    per_head = nch // heads
+
+    def forward(d, right, g):
+        @pl.loop(g * per_head, (g + 1) * per_head)
         def _(k):
             first = (c == 0) if right else (c == n - 1)
 
@@ -185,35 +221,44 @@
 
             rs_copy(d, k, right).start()
 
-    @pl.loop(0, n - 1)
-    def _(t):
-        @pl.when(n - 1 - t > c)
-        def _():
-            x_arrive(n - 1 - t)
-            forward(n - 1 - t, True)
-
-        @pl.when(t < c)
-        def _():
-            x_arrive(t)
-            forward(t, False)
-
-    x_arrive(c)
-
-    @pl.loop(0, nch)
-    def _(k):
-        part[0, k] = dot(c, k)
-
-    @pl.loop(0, nch)
-    def _(k):
-        @pl.when(c > 0)
-        def _():
-            rs_arrive(c, k)
-            part[0, k] += recv[c, k].astype(f32)
-
-        @pl.when(c < n - 1)
-        def _():
-            rs_arrive(n, k)
-            part[0, k] += recv[n, k].astype(f32)
+    for g in range(heads):
+        @pl.loop(0, n - 1)
+        def _(t):
+            @pl.when(n - 1 - t > c)
+            def _():
+                if g == 0:
+                    x_arrive(n - 1 - t)
+                forward(n - 1 - t, True, g)
+
+            @pl.when(t < c)
+            def _():
+                if g == 0:
+                    x_arrive(t)
+                forward(t, False, g)
+
+            if g == heads - 1:
+                pre_step(t)
+
+        if g == 0:
+            x_arrive(c)
+
+    def own(g):
+        @pl.loop(g * per_head, (g + 1) * per_head)
+        def _(k):
+            part[0, k] = dot(c, k)
+
+    def collect(g):
+        @pl.loop(g * per_head, (g + 1) * per_head)
+        def _(k):
+            @pl.when(c > 0)
+            def _():
+                rs_arrive(c, k)
+                part[0, k] += recv[c, k].astype(f32)
+
+            @pl.when(c < n - 1)
+            def _():
+                rs_arrive(n, k)
+                part[0, k] += recv[n, k].astype(f32)
 
     cosines = cos_ref[...]
     sines = sin_ref[...]
@@ -226,24 +271,21 @@
     def turned(v):
         return v * cosines + pltpu.roll(v, HEAD_DIM // 2, 1) * sines
 
-    for g in range(heads):
+    def publish(g):
         newkv[c, g, :, :HEAD_DIM] = turned(piece_of(g, GROUP)).astype(jnp.bfloat16)
         newkv[c, g, :, HEAD_DIM:] = piece_of(g, GROUP + 1).astype(jnp.bfloat16)
-    for o in range(1, n):
-        new_copy(o).start()
-    for g in range(heads):
+        for o in range(1, n):
+            new_copy(o, g).start()
         for j in range(GROUP):
             qbuf[g, j * rows:(j + 1) * rows] = turned(piece_of(g, j)).astype(jnp.bfloat16)
 
-    for o in range(1, n):
-        src = lax.rem(c + o, n)
-        dev = {"ctx": src}
-        rcopy(meta.at[src], meta.at[src], meta_s.at[o], meta_r.at[src], dev).wait_recv()
-        rcopy(pre.at[src], pre.at[src], pre_s.at[o], pre_r.at[src], dev).wait_recv()
-    for o in range(1, n):
-        src = lax.rem(c + o, n)
-        dev = {"ctx": src}
-        rcopy(newkv.at[src], newkv.at[src], new_s.at[o], new_r.at[src], dev).wait_recv()
+    def new_arrive(g):
+        for o in range(1, n):
+            src = lax.rem(c + o, n)
+            rcopy(
+                newkv.at[src, g], newkv.at[src, g], new_s.at[o, g], new_r.at[src, g],
+                {"ctx": src},
+            ).wait_recv()
 
     tile = sbuf.shape[1]
     per_tile = tile // rows
@@ -251,10 +293,8 @@
     nt = (((1,), (1,)), ((), ()))
     unroll = n <= 4
 
-    @pl.loop(0, heads * GROUP // per_tile)
-    def _(i):
-        g = i // (GROUP // per_tile)
-        jj = lax.rem(i, GROUP // per_tile)
+    def one_tile(g, jj):
+        i = g * (GROUP // per_tile) + jj
         q = qbuf[g, pl.ds(pl.multiple_of(jj * tile, 128), tile)]
 
         def scores(b, top):
@@ -299,7 +339,13 @@
             att_ref[:, pl.ds(col, HEAD_DIM)] = out[z * rows:(z + 1) * rows]
 
     slots = dec_ref.shape[1] // BLK
-    for g in range(heads):
+
+    def attend(g):
+        @pl.loop(0, GROUP // per_tile)
+        def _(jj):
+            one_tile(g, jj)
+
+    def place(g):
         for q in range(slots):
             def pick(b, now):
                 hit = meta[b, 1:2, 0:1] == c * slots + q
@@ -310,27 +356,55 @@
             )
             dec_ref[g, q * BLK:(q + 1) * BLK] = found.astype(jnp.bfloat16)
 
+    for o in range(1, n):
+        src = lax.rem(c + o, n)
+        rcopy(
+            meta.at[src], meta.at[src], meta_s.at[o], meta_r.at[src], {"ctx": src}
+        ).wait_recv()
+    own(0)
+    collect(0)
+    publish(0)
+    for g in range(1, heads):
+        own(g)
+        new_arrive(g - 1)
+        attend(g - 1)
+        collect(g)
+        publish(g)
+        place(g - 1)
+    new_arrive(heads - 1)
+    attend(heads - 1)
+    place(heads - 1)
+
     for o in range(1, nhs):
         ss_copy(o).wait_send()
     for j in range(r):
-        @pl.when(hs * r + j != c)
-        def _():
-            st_copy(j).wait_send()
+        for p in range(nh):
+            @pl.when(jnp.logical_not(here(j, p)))
+            def _():
+                st_copy(j, p).wait_send()
     for o in range(1, n):
         meta_copy(o).wait_send()
-        pre_copy(o).wait_send()
-        new_copy(o).wait_send()
+        for g in range(heads):
+            new_copy(o, g).wait_send()
+
+    @pl.loop(0, n)
+    def _(b):
+        @pl.when(jnp.logical_and(b <= c, c < n - 1))
+        def _():
+            pre_copy(b, True).wait_send()
+
+        @pl.when(jnp.logical_and(b >= c, c > 0))
+        def _():
+            pre_copy(b, False).wait_send()
 
     @pl.when(s == root_s)
     def _():
         @pl.loop(0, n)
         def _(d):
-            @pl.when(h == root_h)
-            def _():
-                for o in range(1, nh):
-                    x_copy(d, o).wait_send()
-
-            x_copy(d, 0).wait_send()
+            for o in range(1, nh):
+                x_copy(d, h, o).wait_send()
+            for p in range(nh):
+                x_copy(d, p, 0).wait_send()
 
     @pl.loop(0, n)
     def _(d):
@@ -384,8 +458,8 @@
         out_specs=(vmem, vmem),
         scratch_shapes=[
             pltpu.VMEM((nhs, rows, 128), jnp.float32),
-            pltpu.VMEM((n // nhs, rows, fw), bf16),
-            pltpu.VMEM((n, rows, fw), bf16),
+            pltpu.VMEM((n // nhs, nh, rows // nh, fw), bf16),
+            pltpu.VMEM((n, nh, rows // nh, fw), bf16),
             pltpu.VMEM(w_qkv.shape, bf16),
             pltpu.VMEM((1, nch, rows, CW), jnp.float32),
             pltpu.VMEM((n, nch, rows, CW), wire),
@@ -397,10 +471,10 @@
             pltpu.VMEM((n, tile, prow + rows), jnp.float32),
             dma, dma,
             dma((nhs,)), dma((nhs,)),
-            dma((n // nhs,)),
-            dma((n, nh)), dma((n,)),
+            dma((n // nhs, nh)),
+            dma((n, nh, nh)), dma((n, nh)),
             dma((n, nch)), dma((n + 1, nch)),
-            dma((n,)), dma((n,)), dma((n,)), dma((n,)), dma((n,)), dma((n,)),
+            dma((2, n)), dma((n,)), dma((n, heads)), dma((n, heads)), dma((n,)), dma((n,)),
         ],
         compiler_params=pltpu.CompilerParams(
             collective_id=0, has_side_effects=True, vmem_limit_bytes=56 * 1024 * 1024

time: 225 us -> 208 us (0.924); the launches traced: 225 us -> 204 us
  Pallas kernels: 213 us -> 192 us
    pallas_call x1, Pallas kernels: 213 us -> 192 us  [local(): pl.pallas_call(functools.partial(kernel, n, nh, ns, wire), out_shape=(jax...]
where the time goes in v3:
time: 208 us; the launch traced here: 204 us
  Pallas kernels  192 us (92%)
  local copies, waits for them, and re-layouts  8.17 us (4%)
  between operations  2.61 us (1%)
    pallas_call x1, Pallas kernels, local(): pl.pallas_call(functools.partial(kernel, n, nh, ns, wire), out_shape=(jax...  192 us
    unnamed x3, local copies, waits for them, and re-layouts  6.16 us

profile of v3, /device:TPU:0, one launch (start us, length us, event | category | flops | bytes accessed | tf_op | source)
XLA Modules:
  0.0 204.3 jit_solution(3749171217098896285)
XLA Ops:
  2.6 0.7 concatenate.12.meta_in
  3.3 1.4 reshape.25.gain_ref
  4.6 0.3 fusion
  4.9 0.7 pad_maximum_fusion
  5.7 1.9 copy.12
  7.6 192.5 %shard_map.86 = (bf16[128,2048]{1,0:T(8,128)(2,1)}, bf16[2,512,256]{2,1,0:T(8,128)(2,1)}) custom-call(bf16[128,2048]{1,0:T(8,128)(2,1)} %tok_ref.1, bf16[1,8192]{1,0:T(2,128)(2,1)} %reshape.25.gain_ref, bf16[2048,2560]{1,0:T(8,128)(2,1)} %w_hbm.1, bf16[2,512,256]{2,1,0:T(8,128)(2,1)} %bitcast.8, s32[8,128]{1,0:T(8,128)} %concatenate.12.meta_in, ...), custom_call_target="tpu_custom_call" | custom-call | tf_op jit(solution)/shard_map/pallas_call | solution.py:451
  200.1 2.4 %copy.10 = bf16[512,2,256]{2,1,0:T(2,128)(2,1)} copy(bf16[512,2,256]{2,0,1:T(8,128)(2,1)} %bitcast.9) | data formatting | bytes 1048576
  202.5 1.9 copy.17
  (3 shorter events, 0.0 us)

commit v4 on v3

--- a/solution.py
+++ b/solution.py
@@ -13,7 +13,7 @@
 BLK = 128
 ROPE_BASE = 500000.0
 NORM_EPS = 1e-05
-CW = 640
+CW = 256
 MESH = pl.DeviceIdType.MESH
 
 

time: 208 us -> 202 us (0.971)
  Pallas kernels: 192 us -> 186 us
    pallas_call x1, Pallas kernels: 192 us -> 186 us  [local(): pl.pallas_call(functools.partial(kernel, n, nh, ns, wire), out_shape=(jax...]
where the time goes in v4:
time: 202 us; the launch traced here: 198 us
  Pallas kernels  186 us (92%)
  local copies, waits for them, and re-layouts  8.17 us (4%)
  between operations  2.61 us (1%)
    pallas_call x1, Pallas kernels, local(): pl.pallas_call(functools.partial(kernel, n, nh, ns, wire), out_shape=(jax...  186 us
    unnamed x3, local copies, waits for them, and re-layouts  6.16 us

profile of v4, /device:TPU:0, one launch (start us, length us, event | category | flops | bytes accessed | tf_op | source)
XLA Modules:
  0.0 198.1 jit_solution(11143145346915568049)
XLA Ops:
  2.6 0.7 concatenate.12.meta_in
  3.3 1.4 reshape.25.gain_ref
  4.6 0.3 fusion
  4.9 0.7 pad_maximum_fusion
  5.7 1.9 copy.12
  7.6 186.2 %shard_map.86 = (bf16[128,2048]{1,0:T(8,128)(2,1)}, bf16[2,512,256]{2,1,0:T(8,128)(2,1)}) custom-call(bf16[128,2048]{1,0:T(8,128)(2,1)} %tok_ref.1, bf16[1,8192]{1,0:T(2,128)(2,1)} %reshape.25.gain_ref, bf16[2048,2560]{1,0:T(8,128)(2,1)} %w_hbm.1, bf16[2,512,256]{2,1,0:T(8,128)(2,1)} %bitcast.8, s32[8,128]{1,0:T(8,128)} %concatenate.12.meta_in, ...), custom_call_target="tpu_custom_call" | custom-call | tf_op jit(solution)/shard_map/pallas_call | solution.py:451
  193.8 2.4 %copy.10 = bf16[512,2,256]{2,1,0:T(2,128)(2,1)} copy(bf16[512,2,256]{2,0,1:T(8,128)(2,1)} %bitcast.9) | data formatting | bytes 1048576
  196.2 1.9 copy.17
  (3 shorter events, 0.0 us)
